TPU v7x, 32 devices: a whole 2x2x4 slice. The times are simulated.
32 devices in a mesh: wide: 4 (over y, core), narrow: 4 (over z), net: 2 (over x).
Axes of the slice: x: 2, y: 2, z: 4, core: 2. Of those that a mesh axis runs over, the one named last changes fastest.
Arguments:
- fields: float32 [4, 16, 16, 1024], P(None, 'net', 'wide', 'narrow'), may hold values from -7.5 to 7.5
- conv1_weight: bfloat16 [27, 32, 4], replicated, may hold values from -0.625 to 0.625
- conv1_bias: float32 [32], replicated, may hold values from -6 to 6
- conv2_weight: bfloat16 [27, 6, 32], replicated, may hold values from -0.21875 to 0.21875
Outputs:
- advanced: float32 [4, 16, 16, 1024], P(None, 'net', 'wide', 'narrow')
All inputs are finite; a program needn't handle non-finite values.
Results may differ from a plain program's by a relative error of at most 0.0028.
Values may be sent and summed in bfloat16 or wider, within the bound.
A program may use at most 64 MiB of HBM per device.

v0:
```python
import functools
import math

import jax
import jax.numpy as jnp
import numpy as np
from jax import lax
from jax.experimental import pallas as pl
from jax.experimental.pallas import tpu as pltpu
from jax.sharding import PartitionSpec as P

MESH = pl.DeviceIdType.MESH
TIME_STEP = 0.2
VISCOSITY = 0.05
EDGE = 128


def gather_kernel(nets, wides, narrows, own_ref, main_ref, edge_ref, after, before, packed,
                  y_send, y_recv, main_send, main_recv, edge_send, edge_recv, local_sem):
    net, wide, narrow = lax.axis_index("net"), lax.axis_index("wide"), lax.axis_index("narrow")
    up, down = lax.rem(narrow + 1, narrows), lax.rem(narrow + narrows - 1, narrows)
    length = own_ref.shape[1]
    offsets = [(dn, dw) for dn in range(nets) for dw in range(wides) if (dn, dw) != (0, 0)]

    def device(n, w, k):
        return {"net": n, "wide": w, "narrow": k}

    def target(dn, dw):
        return device(lax.rem(net + nets - dn, nets), lax.rem(wide + wides - dw, wides), narrow)

    barrier = pltpu.get_barrier_semaphore()
    for k in (up, down):
        pl.semaphore_signal(barrier, inc=1, device_id=device(net, wide, k), device_id_type=MESH)
    for dn, dw in offsets:
        pl.semaphore_signal(barrier, inc=1, device_id=target(dn, dw), device_id_type=MESH)
    pl.semaphore_wait(barrier, 2 + len(offsets))

    def remote(src, dst, send, recv, where):
        return pltpu.make_async_remote_copy(
            src_ref=src, dst_ref=dst, send_sem=send, recv_sem=recv, device_id=where, device_id_type=MESH
        )

    to_down = remote(own_ref.at[:, pl.ds(0, EDGE)], after, y_send.at[0], y_recv.at[0], device(net, wide, down))
    to_up = remote(own_ref.at[:, pl.ds(length - EDGE, EDGE)], before, y_send.at[1], y_recv.at[1], device(net, wide, up))
    to_down.start()
    to_up.start()
    mains = []
    for dn, dw in offsets:
        slot = dn * wides + dw
        mains.append(remote(own_ref, main_ref.at[slot], main_send.at[slot], main_recv.at[slot], target(dn, dw)))
        mains[-1].start()
    own_main = pltpu.make_async_copy(own_ref, main_ref.at[0], local_sem.at[0])
    own_main.start()
    to_down.wait()
    to_up.wait()
    lane = lax.broadcasted_iota(jnp.int32, after.shape, 1)
    packed[...] = jnp.where(
        lane < EDGE // 2, after[...].astype(jnp.float32), before[...].astype(jnp.float32)
    ).astype(packed.dtype)
    edges = []
    for dn, dw in offsets:
        slot = dn * wides + dw
        edges.append(remote(packed, edge_ref.at[slot], edge_send.at[slot], edge_recv.at[slot], target(dn, dw)))
        edges[-1].start()
    own_edge = pltpu.make_async_copy(packed, edge_ref.at[0], local_sem.at[1])
    own_edge.start()
    for copy in mains + edges + [own_main, own_edge]:
        copy.wait()


def gather(own, nets, wides, narrows):
    rows, length = own.shape
    slots = nets * wides
    return pl.pallas_call(
        functools.partial(gather_kernel, nets, wides, narrows),
        out_shape=[
            jax.ShapeDtypeStruct((slots, rows, length), own.dtype),
            jax.ShapeDtypeStruct((slots, rows, EDGE), own.dtype),
        ],
        in_specs=[pl.BlockSpec(memory_space=pltpu.VMEM)],
        out_specs=[pl.BlockSpec(memory_space=pl.ANY)] * 2,
        scratch_shapes=[
            pltpu.VMEM((rows, EDGE), own.dtype),
            pltpu.VMEM((rows, EDGE), own.dtype),
            pltpu.VMEM((rows, EDGE), own.dtype),
            pltpu.SemaphoreType.DMA((2,)),
            pltpu.SemaphoreType.DMA((2,)),
            pltpu.SemaphoreType.DMA((slots,)),
            pltpu.SemaphoreType.DMA((slots,)),
            pltpu.SemaphoreType.DMA((slots,)),
            pltpu.SemaphoreType.DMA((slots,)),
            pltpu.SemaphoreType.DMA((2,)),
        ],
        compiler_params=pltpu.CompilerParams(collective_id=0, has_side_effects=True),
    )(own)


def shifted(values, offset, axis):
    return pltpu.roll(values, (-offset) % values.shape[axis], axis)


def two_parts(values):
    high = values.astype(jnp.bfloat16)
    low = (values - high.astype(jnp.float32)).astype(jnp.bfloat16)
    return high, low


def gelu(x):
    inner = x * (0.7978845608028654 + 0.035677408136300125 * (x * x))
    half = 0.5 * x
    return half + half * jnp.tanh(inner)


def step_kernel(nets, wides, main_ref, edge_ref, own_ref, w1_ref, bias_ref, w2_ref, pool_ref, spread_ref,
                out_ref, base, state, thin, taps, wide_hidden, partial, turned, upper, force, mains, edges, arrived):
    fields, xs, depth, lanes = own_ref.shape
    big_x, big_z, ring = base.shape[1:]
    coarse_x, coarse_z = big_x // 2, big_z // 2
    coarse_ring = pool_ref.shape[0]
    block = fields * big_z
    part_x = thin.shape[0] // block
    stage = mains.shape[0]
    unroll = 2 if big_z <= 16 else 1
    variants, window = w1_ref.shape[0], w1_ref.shape[2]
    pad = (taps.shape[2] - coarse_x * block) // 2
    channels = w2_ref.shape[1]
    width = w2_ref.shape[2] // 3
    batch = wide_hidden.shape[0]
    together = max(1, 128 // width)

    for begin in range(0, nets * wides, stage):
        copies = [
            pltpu.make_async_copy(main_ref.at[pl.ds(begin, stage)], mains, arrived.at[0]),
            pltpu.make_async_copy(edge_ref.at[pl.ds(begin, stage)], edges, arrived.at[1]),
        ]
        for copy in copies:
            copy.start()
        for copy in copies:
            copy.wait()
        for i in range(stage):
            dn, dw = divmod(begin + i, wides)
            x_at, z_at = pl.ds(dw * xs, xs), pl.ds(dn * depth, depth)
            if begin + i == 0:
                base[:, x_at, z_at, pl.ds(0, lanes)] = own_ref[...]
            else:
                base[:, x_at, z_at, pl.ds(0, lanes)] = (
                    mains[i].astype(jnp.float32).reshape(fields, xs, depth, lanes)
                )
            base[:, x_at, z_at, pl.ds(lanes, EDGE)] = (
                edges[i].astype(jnp.float32).reshape(fields, xs, depth, EDGE)
            )

    def each(count, body):
        if count == 1:
            body(0)
        else:
            pl.loop(0, count)(body)

    def wrapped(i, size):
        return (i + size) % size if isinstance(i, int) else lax.rem(i + size, size)

    def forces(src):
        @functools.partial(each, coarse_x // part_x)
        def _(turn):
            chunk = turn * part_x

            @pl.loop(0, part_x, unroll=unroll)
            def _(i):
                x = chunk + i
                for c in range(fields):
                    both = src[c, 2 * x] + src[c, 2 * x + 1]
                    both = both + shifted(both, 1, 0)
                    high, low = two_parts(both)
                    at = pl.ds(pl.multiple_of(i * block + c * big_z, big_z), big_z)
                    thin[at, pl.ds(0, ring)] = high
                    thin[at, pl.ds(ring, ring)] = low

            coarse = lax.dot_general(
                pool_ref[...], thin[...], (((1,), (1,)), ((), ())), preferred_element_type=jnp.float32
            )
            for dy in range(3):
                moved = (coarse if dy == 1 else shifted(coarse, dy - 1, 0)).astype(jnp.bfloat16)
                at = pl.multiple_of(pad + chunk * block, 128)
                taps[dy, :, pl.ds(at, part_x * block)] = moved

        span = coarse_x * block
        taps[:, :, pl.ds(0, pad)] = taps[:, :, pl.ds(span, pad)]
        taps[:, :, pl.ds(pad + span, pad)] = taps[:, :, pl.ds(pad, pad)]

        if batch < coarse_x:
            partial[...] = jnp.zeros_like(partial)

        @functools.partial(each, coarse_x // batch)
        def _(turn):
            begin = turn * batch
            for variant in range(variants):
                mine = list(range(variant, batch, variants))
                rows = []
                for x in mine:
                    at = pl.multiple_of(begin * block + (pad + (x - 1) * block) // 128 * 128, 128)
                    rows.append(jnp.concatenate([taps[dy, :, pl.ds(at, window)] for dy in range(3)], axis=1))
                around = jnp.concatenate(rows, axis=0)
                weight = w1_ref[variant].reshape(3 * window, channels)
                hidden = jnp.dot(around, weight, preferred_element_type=jnp.float32) + bias_ref[...]
                hidden = gelu(hidden)
                for i, x in enumerate(mine):
                    here = hidden[i * coarse_ring : (i + 1) * coarse_ring]
                    for dy in range(3):
                        moved = (here if dy == 1 else shifted(here, dy - 1, 0)).astype(jnp.bfloat16)
                        wide_hidden[x, :, pl.ds(dy * channels, channels)] = moved
            found = jnp.dot(
                wide_hidden[...].reshape(batch * coarse_ring, 3 * channels),
                w2_ref[...].reshape(3 * channels, 3 * width),
                preferred_element_type=jnp.float32,
            )
            found = found.reshape(batch, coarse_ring, 3 * width)
            for i in range(batch):
                if batch == coarse_x:
                    total = found[(i - 1) % coarse_x, :, :width] + found[i, :, width : 2 * width]
                    partial[i] = total + found[(i + 1) % coarse_x, :, 2 * width :]
                else:
                    for dx in range(3):
                        partial[wrapped(begin + i + 1 - dx, coarse_x)] += found[i, :, dx * width : (dx + 1) * width]

        def turn_over(x):
            totals = [partial[x + i] for i in range(together)]
            total = jnp.concatenate(totals, axis=1) if together > 1 else totals[0]
            at = x * width if isinstance(x, int) else pl.multiple_of(x * width, width)
            turned[pl.ds(at, together * width), :] = total.T.astype(jnp.bfloat16)

        if batch == coarse_x:
            for x in range(0, coarse_x, together):
                turn_over(x)
        else:
            pl.loop(0, coarse_x // together)(lambda i: turn_over(i * together))

        @functools.partial(each, coarse_x // batch)
        def _(turn):
            begin = turn * batch
            at = pl.multiple_of(begin * width, batch * width)
            fine = jnp.dot(
                turned[pl.ds(at, batch * width), :], spread_ref[...], preferred_element_type=jnp.float32
            )
            upper[pl.ds(begin, batch)] = fine.reshape(batch, width, ring)

        @pl.loop(0, coarse_x, unroll=unroll)
        def _(x):
            ahead, behind = wrapped(x + 1, coarse_x), wrapped(x - 1, coarse_x)

            def part(at, component):
                return upper[at, pl.ds(component * coarse_z, coarse_z)]

            for axis, (in_x, in_y, in_z) in enumerate(((0, 3, 4), (3, 1, 5), (4, 5, 2))):
                along_y, along_z = part(x, in_y), part(x, in_z)
                total = part(ahead, in_x) - part(behind, in_x)
                total = total + shifted(along_y, 2, 1) - shifted(along_y, -2, 1)
                total = 0.25 * (total + shifted(along_z, 1, 0) - shifted(along_z, -1, 0))
                force[x, axis] = jnp.broadcast_to(total[:, None], (coarse_z, 2, ring)).reshape(big_z, ring)

    def rates(src, x, give):
        ahead, behind = wrapped(x + 1, big_x), wrapped(x - 1, big_x)
        half = [0.5 * src[c, x] for c in range(3)]
        u, v, w = half
        plus = [VISCOSITY - h for h in half]
        minus = [VISCOSITY + h for h in half]
        for c in range(fields):
            q = src[c, x]
            rate = plus[0] * src[c, ahead] + minus[0] * src[c, behind]
            rate = rate + plus[1] * shifted(q, 1, 1) + minus[1] * shifted(q, -1, 1)
            rate = rate + plus[2] * shifted(q, 1, 0) + minus[2] * shifted(q, -1, 0)
            rate = rate - (6.0 * VISCOSITY) * q
            if c < 3:
                rate = rate + force[x // 2, c]
            give(c, q, rate)

    forces(base)

    @pl.loop(0, big_x, unroll=unroll)
    def _(x):
        def give(c, q, rate):
            state[c, x] = q + TIME_STEP * rate

        rates(base, x, give)

    forces(state)

    @pl.loop(0, big_x, unroll=unroll)
    def _(x):
        def give(c, q, rate):
            base[c, x] = 0.75 * base[c, x] + 0.25 * (q + TIME_STEP * rate)

        rates(state, x, give)

    forces(base)

    for x in range(xs):
        def give(c, q, rate):
            moved = (q + TIME_STEP * rate)[:depth, :lanes]
            out_ref[c, x] = own_ref[c, x] * (1.0 / 3.0) + (2.0 / 3.0) * moved

        rates(base, x, give)


def step(main, edge, own, w1, bias, w2, pool, spread, nets, wides):
    fields, xs, depth, lanes = own.shape
    big_x, big_z, ring = xs * wides, depth * nets, lanes + EDGE
    coarse_x, coarse_ring = big_x // 2, pool.shape[0]
    block = fields * big_z
    part_x = math.gcd(coarse_x, max(1, 512 // block))
    stage = math.gcd(nets * wides, 8)
    batch = math.gcd(coarse_x, 8 if block < 128 else 1)
    channels, width = w2.shape[1], w2.shape[2] // 3
    return pl.pallas_call(
        functools.partial(step_kernel, nets, wides),
        out_shape=jax.ShapeDtypeStruct(own.shape, jnp.float32),
        in_specs=[pl.BlockSpec(memory_space=pl.ANY)] * 2 + [pl.BlockSpec(memory_space=pltpu.VMEM)] * 6,
        out_specs=pl.BlockSpec(memory_space=pltpu.VMEM),
        scratch_shapes=[
            pltpu.VMEM((fields, big_x, big_z, ring), jnp.float32),
            pltpu.VMEM((fields, big_x, big_z, ring), jnp.float32),
            pltpu.VMEM((part_x * block, 2 * ring), jnp.bfloat16),
            pltpu.VMEM((3, coarse_ring, coarse_x * block + 2 * max(128, block)), jnp.bfloat16),
            pltpu.VMEM((batch, coarse_ring, 3 * channels), jnp.bfloat16),
            pltpu.VMEM((coarse_x, coarse_ring, width), jnp.float32),
            pltpu.VMEM((coarse_x * width, coarse_ring), jnp.bfloat16),
            pltpu.VMEM((coarse_x, width, ring), jnp.float32),
            pltpu.VMEM((coarse_x, 3, big_z, ring), jnp.float32),
            pltpu.VMEM((stage, *main.shape[1:]), main.dtype),
            pltpu.VMEM((stage, *edge.shape[1:]), edge.dtype),
            pltpu.SemaphoreType.DMA((2,)),
        ],
        compiler_params=pltpu.CompilerParams(vmem_limit_bytes=60 * 1024 * 1024),
    )(main, edge, own, w1, bias, w2, pool, spread)


HALO = 16


def constants(lanes, big_z, fields):
    ring, own, coarse_z = lanes + EDGE, lanes // 2, big_z // 2
    coarse_ring = own + 2 * HALO
    covers = np.zeros((coarse_ring, ring), np.float32)
    for m in range(coarse_ring):
        first = 2 * m if m < own + HALO else ring - 2 * (coarse_ring - m)
        covers[m, first : first + 2] = 1.0
    pool = np.concatenate([covers, covers], 1) * 0.125
    block = fields * big_z
    group = max(1, 128 // block)
    slots = 3 if group == 1 else 2 * group
    first = np.zeros((big_z, coarse_z, 3), np.float32)
    second = np.zeros((coarse_z, coarse_z, 3), np.float32)
    for dz in range(3):
        for z in range(coarse_z):
            first[2 * ((z + dz - 1) % coarse_z), z, dz] = 1.0
            second[(z + dz - 1) % coarse_z, z, dz] = 1.0
    places = np.zeros((group, slots, 3), np.float32)
    for variant in range(group):
        for dx in range(3):
            places[variant, (variant - 1) % group + dx, dx] = 1.0
    return [jnp.asarray(a, jnp.bfloat16) for a in (pool, covers, first, second, places)]


def per_device(nets, wides, narrows, fields, conv1_weight, conv1_bias, conv2_weight):
    count, depth, xs, lanes = fields.shape
    big_z = depth * nets
    coarse_z = big_z // 2
    pool, spread, first, second, places = constants(lanes, big_z, count)
    own = fields.transpose(0, 2, 1, 3)
    main, edge = gather(own.astype(jnp.bfloat16).reshape(-1, lanes), nets, wides, narrows)
    hidden, channels = conv1_weight.shape[1:]
    parts = conv2_weight.shape[1]
    w1 = conv1_weight.reshape(3, 3, 3, hidden, channels)
    w1 = jnp.einsum("dxyoc,qpd,vsx->vyscqpo", w1, first, places)
    w1 = w1.reshape(places.shape[0], 3, places.shape[1] * channels * big_z, coarse_z * hidden)
    w2 = jnp.einsum("dxysh,qpd->yqhxsp", conv2_weight.reshape(3, 3, 3, parts, hidden), second)
    w2 = w2.reshape(3, coarse_z * hidden, 3, parts * coarse_z)
    width = parts * coarse_z
    width = 64 if width <= 64 else -(-width // 128) * 128
    w2 = jnp.pad(w2, ((0, 0), (0, 0), (0, 0), (0, width - parts * coarse_z))).reshape(3, coarse_z * hidden, 3 * width)
    bias = jnp.tile(conv1_bias, coarse_z)[None]
    moved = step(main, edge, own, w1, bias, w2, pool, spread, nets, wides)
    return moved.transpose(0, 2, 1, 3)


def solution(mesh):
    in_specs = (P(None, "net", "wide", "narrow"), P(), P(), P())
    out_specs = P(None, "net", "wide", "narrow")
    sizes = (mesh.shape["net"], mesh.shape["wide"], mesh.shape["narrow"])
    return jax.shard_map(
        functools.partial(per_device, *sizes), mesh=mesh, in_specs=in_specs, out_specs=out_specs, check_vma=False
    )
```

profile of v0, /device:TPU:0, one launch (start us, length us, event | category | flops | bytes accessed | tf_op | source)
XLA Modules:
  0.0 50.0 jit_solution(10774667322480618850)
XLA Ops:
  0.0 0.0 copy-start
  0.0 1.6 %copy.40 = bf16[4,8,4,256]{3,1,2,0:T(8,128)(2,1)} copy(f32[4,8,4,256]{3,2,1,0:T(4,128)} %param.9) | data formatting | bytes 196608 | tf_op args[0]
  1.6 17.3 %shard_map.91 = (bf16[8,128,256]{2,1,0:T(8,128)(2,1)}, bf16[8,128,128]{2,1,0:T(8,128)(2,1)}) custom-call(bf16[128,256]{1,0:T(8,128)(2,1)} %bitcast.45), custom_call_target="tpu_custom_call" | custom-call | tf_op jit(solution)/shard_map/pallas_call | solution.py:74
  18.9 0.0 copy-done
  18.9 0.8 %convolution_bitcast_fusion.2 = bf16[2,4,3,3,32,4,1]{4,1,5,3,2,0,6:T(4,128)(2,1)S(1)} fusion(bf16[2,4,3,1,1,1]{2,1,5,4,3,0:T(4,128)(2,1)} %constant.20, bf16[3,3,3,32,4,1]{3,4,2,1,0,5:T(4,128)(2,1)S(1)} %bitcast.41), kind=kOutput, calls=%fused_computation.2 | convolution fusion | flops 55296 | bytes 25392 | tf_op jit(solution)/shard_map/dxyoc,qpd,vsx->vyscqpo/dot_general | solution.py:373
  19.7 1.7 %convolution_bitcast_fusion = bf16[2,3,4,4,16,8,32]{6,4,5,3,1,2,0:T(8,128)(2,1)S(1)} fusion(bf16[16,8,3,1,1,1,1]{0,2,1,6,5,4,3:T(4,128)(2,1)} %constant.21, bf16[2,4,3,3,32,4,1]{4,1,5,3,2,0,6:T(4,128)(2,1)S(1)} %convolution_bitcast_fusion.2), kind=kOutput, calls=%fused_computation | convolution fusion | flops 2359296 | bytes 805632 | tf_op jit(solution)/shard_map/dxyoc,qpd,vsx->vyscqpo/dot_general | solution.py:373
  21.4 1.3 %copy.15 = bf16[2,3,4,4,16,8,32]{6,5,4,3,2,1,0:T(8,128)(2,1)S(1)} copy(bf16[2,3,4,4,16,8,32]{6,4,5,3,1,2,0:T(8,128)(2,1)S(1)} %convolution_bitcast_fusion) | data formatting | bytes 1572864 | tf_op jit(solution)/shard_map/dxyoc,qpd,vsx->vyscqpo/transpose | solution.py:373
  22.7 0.0 copy-start.2
  22.7 0.0 copy-start.3
  22.8 3.0 %reshape.21.w1_ref = bf16[2,3,256,256]{3,2,1,0:T(8,128)(2,1)} reshape(bf16[2,3,4,4,16,8,32]{6,5,4,3,2,1,0:T(8,128)(2,1)S(1)} %copy.15) | data formatting | bytes 1572864 | tf_op jit(solution)/shard_map/reshape | solution.py:374
  25.8 0.0 copy-done.2
  25.8 0.0 copy-start.1
  25.8 0.0 copy-start.4
  25.8 0.0 copy-done.3
  25.8 0.4 convolution_bitcast_fusion.1
  26.3 0.2 copy.17
  26.5 0.6 %reshape.23 = bf16[3,256,3,48]{1,3,2,0:T(8,128)(2,1)S(1)} reshape(bf16[3,8,32,3,6,8]{2,1,5,4,3,0:T(8,128)(2,1)S(1)} %copy.17) | data formatting | bytes 442368 | tf_op jit(solution)/shard_map/reshape | solution.py:376
  27.1 0.9 %copy.18.w2_ref = bf16[3,256,192]{2,1,0:T(8,128)(2,1)} copy(bf16[3,256,192]{1,2,0:T(8,128)(2,1)S(1)} %bitcast.42) | data formatting | bytes 589824 | tf_op jit(solution)/shard_map/reshape | solution.py:379
  28.1 0.0 copy-done.1
  28.1 0.7 %copy.39 = f32[4,8,4,256]{3,1,2,0:T(8,128)} copy(f32[4,8,4,256]{3,2,1,0:T(4,128)S(1)} %copy-done.1) | data formatting | bytes 262144 | tf_op args[0]
  28.8 0.0 copy-done.4
  28.8 0.7 %broadcast_in_dim_tile.3.bias_ref = f32[1,256]{1,0:T(1,128)} reshape(f32[8,32]{1,0:T(8,128)S(1)} %tile.2) | data formatting | bytes 2048 | tf_op jit(solution)/shard_map/broadcast_in_dim;tile | solution.py:380
  29.4 18.9 %shard_map.92 = f32[4,4,8,256]{3,2,1,0:T(8,128)} custom-call(bf16[8,128,256]{2,1,0:T(8,128)(2,1)} %get-tuple-element.7.main_ref, bf16[8,128,128]{2,1,0:T(8,128)(2,1)} %get-tuple-element.8.edge_ref, f32[4,4,8,256]{3,2,1,0:T(8,128)} %bitcast.43, bf16[2,3,256,256]{3,2,1,0:T(8,128)(2,1)} %reshape.21.w1_ref, f32[1,256]{1,0:T(1,128)} %broadcast_in_dim_tile.3.bias_ref, ...), custom_call_target="tpu_custom_call" | custom-call | tf_op jit(solution)/shard_map/pallas_call | solution.py:313
  48.4 1.6 %copy.19 = f32[4,8,4,256]{3,2,1,0:T(4,128)} copy(f32[4,8,4,256]{3,1,2,0:T(8,128)} %bitcast.44) | data formatting | bytes 262144 | tf_op jit(solution)/shard_map/transpose | solution.py:382
  (3 shorter events, 0.1 us)
Async XLA Ops:
  0.0 18.9 %copy-start = (bf16[27,32,4]{1,2,0:T(4,128)(2,1)S(1)}, bf16[27,32,4]{1,2,0:T(4,128)(2,1)}, u32[]{:S(2)}) copy-start(bf16[27,32,4]{1,2,0:T(4,128)(2,1)} %param.10) | copy-start | bytes 20740
  22.7 3.1 %copy-start.2 = (bf16[27,6,32]{2,0,1:T(8,128)(2,1)S(1)}, bf16[27,6,32]{2,0,1:T(8,128)(2,1)}, u32[]{:S(2)}) copy-start(bf16[27,6,32]{2,0,1:T(8,128)(2,1)} %param.12) | copy-start | bytes 31108
  22.7 3.1 %copy-start.3 = (bf16[8,8,3,1,1,1]{1,2,5,4,3,0:T(4,128)(2,1)S(1)}, bf16[8,8,3,1,1,1]{1,2,5,4,3,0:T(4,128)(2,1)}, u32[]{:S(2)}) copy-start(bf16[8,8,3,1,1,1]{1,2,5,4,3,0:T(4,128)(2,1)} %constant.22) | copy-start | bytes 1156
  25.8 2.3 %copy-start.1 = (f32[4,8,4,256]{3,2,1,0:T(4,128)S(1)}, f32[4,8,4,256]{3,2,1,0:T(4,128)}, u32[]{:S(2)}) copy-start(f32[4,8,4,256]{3,2,1,0:T(4,128)} %param.9) | copy-start | bytes 393220
  25.8 3.0 %copy-start.4 = (f32[32]{0:T(128)S(1)}, f32[32]{0:T(128)}, u32[]{:S(2)}) copy-start(f32[32]{0:T(128)} %param.11) | copy-start | bytes 388
where the time goes:
time: 50.3 us; the launch traced here: 50 us
  Pallas kernels  36.2 us (72%)
  local copies, waits for them, and re-layouts  10.7 us (21%)
  matrix products  2.98 us (6%)
    pallas_call x1, Pallas kernels, step(): pl.pallas_call(functools.partial(step_kernel, nets, wides), out_shape=jax...  18.9 us
    pallas_call x1, Pallas kernels, gather(): pl.pallas_call(functools.partial(gather_kernel, nets, wides, narrows), ou...  17.3 us
    reshape x1, local copies, waits for them, and re-layouts, per_device(): w1.reshape(places.shape[0], 3, places.shape[1] * channels * big_z, coarse...  3.03 us
    dot_general x2, matrix products, per_device(): w1 = jnp.einsum('dxyoc,qpd,vsx->vyscqpo', w1, first, places)  2.54 us
    unnamed x12, local copies, waits for them, and re-layouts  2.27 us
    transpose x1, local copies, waits for them, and re-layouts, per_device(): return moved.transpose(0, 2, 1, 3)  1.61 us
    transpose x1, local copies, waits for them, and re-layouts, per_device(): w1 = jnp.einsum('dxyoc,qpd,vsx->vyscqpo', w1, first, places)  1.31 us

commit v1 on v0

--- a/solution.py
+++ b/solution.py
@@ -15,7 +15,49 @@
 EDGE = 128
 
 
-def gather_kernel(nets, wides, narrows, own_ref, main_ref, edge_ref, after, before, packed,
+def joined_weights(conv1_ref, conv2_ref, pick1_ref, pick2_ref, tile_ref, w1_ref, w2_ref, big_z):
+    coarse_z = big_z // 2
+    f32, bf16 = jnp.float32, jnp.bfloat16
+    tile = tile_ref[...]
+    hidden = tile.shape[0]
+    rows, columns = w1_ref.shape[2:]
+    zi = lax.broadcasted_iota(jnp.int32, (rows, columns), 0) % big_z
+    zo = lax.broadcasted_iota(jnp.int32, (rows, columns), 1) // hidden
+    masks1 = [zi == 2 * ((zo + dz + coarse_z - 1) % coarse_z) for dz in range(3)]
+    shape2 = (w2_ref.shape[1], w2_ref.shape[2])
+    width = shape2[1] // 3
+    zi = lax.broadcasted_iota(jnp.int32, shape2, 0) // hidden
+    zo = lax.broadcasted_iota(jnp.int32, shape2, 1) % width % coarse_z
+    masks2 = [zi == (zo + dz + coarse_z - 1) % coarse_z for dz in range(3)]
+
+    def stacked(ref, dz, dy):
+        pieces = []
+        for dx in range(3):
+            piece = ref[9 * dz + 3 * dx + dy].astype(f32)
+            pieces += [piece, jnp.zeros((8 - piece.shape[0], hidden), f32)]
+        return jnp.concatenate(pieces, axis=0).astype(bf16)
+
+    for dy in range(3):
+        total = [None] * w1_ref.shape[0]
+        for dz in range(3):
+            spread = jnp.dot(stacked(conv1_ref, dz, dy), tile, preferred_element_type=f32).astype(bf16)
+            for variant in range(len(total)):
+                term = jnp.dot(pick1_ref[variant], spread, preferred_element_type=f32)
+                term = jnp.where(masks1[dz], term, 0.0)
+                total[variant] = term if dz == 0 else total[variant] + term
+        for variant, value in enumerate(total):
+            w1_ref[variant, dy] = value.astype(bf16)
+        value = None
+        for dz in range(3):
+            repeated = jnp.dot(pick2_ref[...], stacked(conv2_ref, dz, dy), preferred_element_type=f32).astype(bf16)
+            term = lax.dot_general(tile, repeated, (((0,), (1,)), ((), ())), preferred_element_type=f32)
+            term = jnp.where(masks2[dz], term, 0.0)
+            value = term if dz == 0 else value + term
+        w2_ref[dy] = value.astype(bf16)
+
+
+def gather_kernel(nets, wides, narrows, big_z, state_ref, conv1_ref, conv2_ref, pick1_ref, pick2_ref, tile_ref,
+                  main_ref, edge_ref, w1_ref, w2_ref, own_ref, after, before, packed,
                   y_send, y_recv, main_send, main_recv, edge_send, edge_recv, local_sem):
     net, wide, narrow = lax.axis_index("net"), lax.axis_index("wide"), lax.axis_index("narrow")
     up, down = lax.rem(narrow + 1, narrows), lax.rem(narrow + narrows - 1, narrows)
@@ -28,6 +70,7 @@
     def target(dn, dw):
         return device(lax.rem(net + nets - dn, nets), lax.rem(wide + wides - dw, wides), narrow)
 
+    own_ref[...] = state_ref[...].astype(own_ref.dtype)
     barrier = pltpu.get_barrier_semaphore()
     for k in (up, down):
         pl.semaphore_signal(barrier, inc=1, device_id=device(net, wide, k), device_id_type=MESH)
@@ -64,25 +107,31 @@
         edges[-1].start()
     own_edge = pltpu.make_async_copy(packed, edge_ref.at[0], local_sem.at[1])
     own_edge.start()
+    joined_weights(conv1_ref, conv2_ref, pick1_ref, pick2_ref, tile_ref, w1_ref, w2_ref, big_z)
     for copy in mains + edges + [own_main, own_edge]:
         copy.wait()
 
 
-def gather(own, nets, wides, narrows):
+def gather(own, conv1, conv2, picks, width, big_z, nets, wides, narrows):
     rows, length = own.shape
+    travel = jnp.bfloat16
+    columns = picks[2].shape[1]
     slots = nets * wides
     return pl.pallas_call(
-        functools.partial(gather_kernel, nets, wides, narrows),
+        functools.partial(gather_kernel, nets, wides, narrows, big_z),
         out_shape=[
-            jax.ShapeDtypeStruct((slots, rows, length), own.dtype),
-            jax.ShapeDtypeStruct((slots, rows, EDGE), own.dtype),
+            jax.ShapeDtypeStruct((slots, rows, length), travel),
+            jax.ShapeDtypeStruct((slots, rows, EDGE), travel),
+            jax.ShapeDtypeStruct((picks[0].shape[0], 3, picks[0].shape[1], columns), jnp.bfloat16),
+            jax.ShapeDtypeStruct((3, columns, 3 * width), jnp.bfloat16),
         ],
-        in_specs=[pl.BlockSpec(memory_space=pltpu.VMEM)],
-        out_specs=[pl.BlockSpec(memory_space=pl.ANY)] * 2,
+        in_specs=[pl.BlockSpec(memory_space=pltpu.VMEM)] * 6,
+        out_specs=[pl.BlockSpec(memory_space=pl.ANY)] * 2 + [pl.BlockSpec(memory_space=pltpu.VMEM)] * 2,
         scratch_shapes=[
-            pltpu.VMEM((rows, EDGE), own.dtype),
-            pltpu.VMEM((rows, EDGE), own.dtype),
-            pltpu.VMEM((rows, EDGE), own.dtype),
+            pltpu.VMEM((rows, length), travel),
+            pltpu.VMEM((rows, EDGE), travel),
+            pltpu.VMEM((rows, EDGE), travel),
+            pltpu.VMEM((rows, EDGE), travel),
             pltpu.SemaphoreType.DMA((2,)),
             pltpu.SemaphoreType.DMA((2,)),
             pltpu.SemaphoreType.DMA((slots,)),
@@ -91,8 +140,10 @@
             pltpu.SemaphoreType.DMA((slots,)),
             pltpu.SemaphoreType.DMA((2,)),
         ],
-        compiler_params=pltpu.CompilerParams(collective_id=0, has_side_effects=True),
-    )(own)
+        compiler_params=pltpu.CompilerParams(
+            collective_id=0, has_side_effects=True, vmem_limit_bytes=60 * 1024 * 1024
+        ),
+    )(own, conv1, conv2, *picks)
 
 
 def shifted(values, offset, axis):
@@ -127,6 +178,7 @@
     width = w2_ref.shape[2] // 3
     batch = wide_hidden.shape[0]
     together = max(1, 128 // width)
+    bias = jnp.concatenate([bias_ref[...]] * coarse_z, axis=1)
 
     for begin in range(0, nets * wides, stage):
         copies = [
@@ -201,7 +253,7 @@
                     rows.append(jnp.concatenate([taps[dy, :, pl.ds(at, window)] for dy in range(3)], axis=1))
                 around = jnp.concatenate(rows, axis=0)
                 weight = w1_ref[variant].reshape(3 * window, channels)
-                hidden = jnp.dot(around, weight, preferred_element_type=jnp.float32) + bias_ref[...]
+                hidden = jnp.dot(around, weight, preferred_element_type=jnp.float32) + bias
                 hidden = gelu(hidden)
                 for i, x in enumerate(mine):
                     here = hidden[i * coarse_ring : (i + 1) * coarse_ring]
@@ -336,7 +388,7 @@
 HALO = 16
 
 
-def constants(lanes, big_z, fields):
+def constants(lanes, big_z, fields, hidden, parts):
     ring, own, coarse_z = lanes + EDGE, lanes // 2, big_z // 2
     coarse_ring = own + 2 * HALO
     covers = np.zeros((coarse_ring, ring), np.float32)
@@ -347,37 +399,36 @@
     block = fields * big_z
     group = max(1, 128 // block)
     slots = 3 if group == 1 else 2 * group
-    first = np.zeros((big_z, coarse_z, 3), np.float32)
-    second = np.zeros((coarse_z, coarse_z, 3), np.float32)
-    for dz in range(3):
-        for z in range(coarse_z):
-            first[2 * ((z + dz - 1) % coarse_z), z, dz] = 1.0
-            second[(z + dz - 1) % coarse_z, z, dz] = 1.0
-    places = np.zeros((group, slots, 3), np.float32)
+    rows = np.arange(slots * block)
+    slot, channel = rows // block, rows // big_z % fields
+    pick1 = np.zeros((group, slots * block, 24), np.float32)
     for variant in range(group):
         for dx in range(3):
-            places[variant, (variant - 1) % group + dx, dx] = 1.0
-    return [jnp.asarray(a, jnp.bfloat16) for a in (pool, covers, first, second, places)]
+            for c in range(fields):
+                here = (slot == (variant - 1) % group + dx) & (channel == c)
+                pick1[variant, here, 8 * dx + c] = 1.0
+    width = parts * coarse_z
+    width = 64 if width <= 64 else -(-width // 128) * 128
+    pick2 = np.zeros((3 * width, 24), np.float32)
+    for dx in range(3):
+        for s in range(parts):
+            start = dx * width + s * coarse_z
+            pick2[start : start + coarse_z, 8 * dx + s] = 1.0
+    tile = np.tile(np.eye(hidden, dtype=np.float32), (1, coarse_z))
+    return [jnp.asarray(a, jnp.bfloat16) for a in (pool, covers, pick1, pick2, tile)]
 
 
 def per_device(nets, wides, narrows, fields, conv1_weight, conv1_bias, conv2_weight):
     count, depth, xs, lanes = fields.shape
     big_z = depth * nets
-    coarse_z = big_z // 2
-    pool, spread, first, second, places = constants(lanes, big_z, count)
+    hidden, parts = conv1_weight.shape[1], conv2_weight.shape[1]
+    pool, spread, *picks = constants(lanes, big_z, count, hidden, parts)
     own = fields.transpose(0, 2, 1, 3)
-    main, edge = gather(own.astype(jnp.bfloat16).reshape(-1, lanes), nets, wides, narrows)
-    hidden, channels = conv1_weight.shape[1:]
-    parts = conv2_weight.shape[1]
-    w1 = conv1_weight.reshape(3, 3, 3, hidden, channels)
-    w1 = jnp.einsum("dxyoc,qpd,vsx->vyscqpo", w1, first, places)
-    w1 = w1.reshape(places.shape[0], 3, places.shape[1] * channels * big_z, coarse_z * hidden)
-    w2 = jnp.einsum("dxysh,qpd->yqhxsp", conv2_weight.reshape(3, 3, 3, parts, hidden), second)
-    w2 = w2.reshape(3, coarse_z * hidden, 3, parts * coarse_z)
-    width = parts * coarse_z
-    width = 64 if width <= 64 else -(-width // 128) * 128
-    w2 = jnp.pad(w2, ((0, 0), (0, 0), (0, 0), (0, width - parts * coarse_z))).reshape(3, coarse_z * hidden, 3 * width)
-    bias = jnp.tile(conv1_bias, coarse_z)[None]
+    main, edge, w1, w2 = gather(
+        own.reshape(-1, lanes), conv1_weight.transpose(0, 2, 1), conv2_weight, picks,
+        picks[1].shape[0] // 3, big_z, nets, wides, narrows,
+    )
+    bias = conv1_bias[None]
     moved = step(main, edge, own, w1, bias, w2, pool, spread, nets, wides)
     return moved.transpose(0, 2, 1, 3)
 

time: 50.3 us -> 42.3 us (0.84)
  local copies, waits for them, and re-layouts: 10.7 us -> 4.63 us
  matrix products: 2.98 us -> 0 us
  Pallas kernels: 36.2 us -> 37.4 us
    reshape x4 -> x0, local copies, waits for them, and re-layouts: 4.59 us -> none  [the longest x1 3.03 us: per_device(): w1.reshape(places.shape[0], 3, places.shape[1] * channels * big_z, coarse...]
    dot_general x3 -> x0, matrix products: 2.98 us -> none  [the longest x2 2.54 us: per_device(): w1 = jnp.einsum('dxyoc,qpd,vsx->vyscqpo', w1, first, places)]
    transpose x2 -> x0, local copies, waits for them, and re-layouts: 1.54 us -> none  [the longest x1 1.31 us: per_device(): w1 = jnp.einsum('dxyoc,qpd,vsx->vyscqpo', w1, first, places)]
    pallas_call x1, Pallas kernels: 17.3 us -> 18.5 us  [gather(): pl.pallas_call(functools.partial(gather_kernel, nets, wides, narrows, big...]
    unnamed x12 -> x2, local copies, waits for them, and re-layouts: 2.27 us -> 3.02 us
    another operation x2 -> x0, local copies, waits for them, and re-layouts: 0.67 us -> none  [per_device(): bias = jnp.tile(conv1_bias, coarse_z)[None]]
where the time goes in v1:
time: 42.3 us; the launch traced here: 42 us
  Pallas kernels  37.4 us (88%)
  local copies, waits for them, and re-layouts  4.63 us (11%)
    pallas_call x1, Pallas kernels, step(): pl.pallas_call(functools.partial(step_kernel, nets, wides), out_shape=jax...  18.9 us
    pallas_call x1, Pallas kernels, gather(): pl.pallas_call(functools.partial(gather_kernel, nets, wides, narrows, big...  18.5 us
    unnamed x2, local copies, waits for them, and re-layouts  3.02 us
    transpose x1, local copies, waits for them, and re-layouts, per_device(): return moved.transpose(0, 2, 1, 3)  1.61 us

profile of v1, /device:TPU:0, one launch (start us, length us, event | category | flops | bytes accessed | tf_op | source)
XLA Modules:
  0.0 42.0 jit_solution(15232908214700677177)
XLA Ops:
  0.0 1.4 %copy.11.conv2_ref = bf16[27,6,32]{2,1,0:T(8,128)(2,1)} copy(bf16[27,6,32]{2,0,1:T(8,128)(2,1)} %param.12) | data formatting | bytes 20736 | tf_op args[3]
  1.4 1.6 %copy.15 = f32[4,8,4,256]{3,1,2,0:T(8,128)} copy(f32[4,8,4,256]{3,2,1,0:T(4,128)} %param.9) | data formatting | bytes 262144 | tf_op args[0]
  3.0 18.5 %shard_map.91 = (bf16[8,128,256]{2,1,0:T(8,128)(2,1)}, bf16[8,128,128]{2,1,0:T(8,128)(2,1)}, bf16[2,3,256,256]{3,2,1,0:T(8,128)(2,1)}, bf16[3,256,192]{2,1,0:T(8,128)(2,1)}) custom-call(f32[128,256]{1,0:T(8,128)} %bitcast.8, bf16[27,4,32]{2,1,0:T(4,128)(2,1)} %bitcast.11, bf16[27,6,32]{2,1,0:T(8,128)(2,1)} %copy.11.conv2_ref, ...), custom_call_target="tpu_custom_call" | custom-call | tf_op jit(solution)/shard_map/pallas_call | solution.py:120
  21.5 18.9 %shard_map.92 = f32[4,4,8,256]{3,2,1,0:T(8,128)} custom-call(bf16[8,128,256]{2,1,0:T(8,128)(2,1)} %get-tuple-element.9.main_ref, bf16[8,128,128]{2,1,0:T(8,128)(2,1)} %get-tuple-element.10.edge_ref, f32[4,4,8,256]{3,2,1,0:T(8,128)} %bitcast.9, bf16[2,3,256,256]{3,2,1,0:T(8,128)(2,1)} %get-tuple-element.11.w1_ref, f32[1,32]{1,0:T(1,128)} %bitcast.12, ...), custom_call_target="tpu_custom_call" | custom-call | tf_op jit(solution)/shard_map/pallas_call | solution.py:365
  40.4 1.6 %copy.12 = f32[4,8,4,256]{3,2,1,0:T(4,128)} copy(f32[4,8,4,256]{3,1,2,0:T(8,128)} %bitcast.10) | data formatting | bytes 262144 | tf_op jit(solution)/shard_map/transpose | solution.py:433

commit v2 on v1

--- a/solution.py
+++ b/solution.py
@@ -33,14 +33,19 @@
     def stacked(ref, dz, dy):
         pieces = []
         for dx in range(3):
-            piece = ref[9 * dz + 3 * dx + dy].astype(f32)
+            piece = ref(9 * dz + 3 * dx + dy)
             pieces += [piece, jnp.zeros((8 - piece.shape[0], hidden), f32)]
         return jnp.concatenate(pieces, axis=0).astype(bf16)
+
+    second = conv2_ref[...].astype(f32)
+
+    def second_tap(t):
+        return jnp.concatenate([second[i, t : t + 1] for i in range(second.shape[0])], axis=0)
 
     for dy in range(3):
         total = [None] * w1_ref.shape[0]
         for dz in range(3):
-            spread = jnp.dot(stacked(conv1_ref, dz, dy), tile, preferred_element_type=f32).astype(bf16)
+            spread = jnp.dot(stacked(lambda t: conv1_ref[t].astype(f32), dz, dy), tile, preferred_element_type=f32).astype(bf16)
             for variant in range(len(total)):
                 term = jnp.dot(pick1_ref[variant], spread, preferred_element_type=f32)
                 term = jnp.where(masks1[dz], term, 0.0)
@@ -49,7 +54,7 @@
             w1_ref[variant, dy] = value.astype(bf16)
         value = None
         for dz in range(3):
-            repeated = jnp.dot(pick2_ref[...], stacked(conv2_ref, dz, dy), preferred_element_type=f32).astype(bf16)
+            repeated = jnp.dot(pick2_ref[...], stacked(second_tap, dz, dy), preferred_element_type=f32).astype(bf16)
             term = lax.dot_general(tile, repeated, (((0,), (1,)), ((), ())), preferred_element_type=f32)
             term = jnp.where(masks2[dz], term, 0.0)
             value = term if dz == 0 else value + term
@@ -57,12 +62,11 @@
 
 
 def gather_kernel(nets, wides, narrows, big_z, state_ref, conv1_ref, conv2_ref, pick1_ref, pick2_ref, tile_ref,
-                  main_ref, edge_ref, w1_ref, w2_ref, own_ref, after, before, packed,
+                  main_ref, edge_ref, w1_ref, w2_ref, turned_ref, own_ref, after, before, packed,
                   y_send, y_recv, main_send, main_recv, edge_send, edge_recv, local_sem):
     net, wide, narrow = lax.axis_index("net"), lax.axis_index("wide"), lax.axis_index("narrow")
     up, down = lax.rem(narrow + 1, narrows), lax.rem(narrow + narrows - 1, narrows)
     length = own_ref.shape[1]
-    offsets = [(dn, dw) for dn in range(nets) for dw in range(wides) if (dn, dw) != (0, 0)]
 
     def device(n, w, k):
         return {"net": n, "wide": w, "narrow": k}
@@ -70,13 +74,22 @@
     def target(dn, dw):
         return device(lax.rem(net + nets - dn, nets), lax.rem(wide + wides - dw, wides), narrow)
 
-    own_ref[...] = state_ref[...].astype(own_ref.dtype)
+    core = lax.rem(wide, 2)
+    partner = device(net, wide + 1 - 2 * core, narrow)
+    direct = [(dn, dw) for dn in range(nets) for dw in range(0, wides, 2) if (dn, dw) != (0, 0)]
+    handed = [dn * wides + dw for dn in range(nets) for dw in range(1, wides, 2)]
+
     barrier = pltpu.get_barrier_semaphore()
     for k in (up, down):
         pl.semaphore_signal(barrier, inc=1, device_id=device(net, wide, k), device_id_type=MESH)
-    for dn, dw in offsets:
+    for dn, dw in direct:
         pl.semaphore_signal(barrier, inc=1, device_id=target(dn, dw), device_id_type=MESH)
-    pl.semaphore_wait(barrier, 2 + len(offsets))
+    pl.semaphore_signal(barrier, inc=1, device_id=partner, device_id_type=MESH)
+    for f in range(state_ref.shape[0]):
+        for x in range(state_ref.shape[2]):
+            turned_ref[f, x] = state_ref[f, :, x, :]
+    own_ref[...] = turned_ref[...].reshape(own_ref.shape).astype(own_ref.dtype)
+    pl.semaphore_wait(barrier, 3 + len(direct))
 
     def remote(src, dst, send, recv, where):
         return pltpu.make_async_remote_copy(
@@ -87,11 +100,17 @@
     to_up = remote(own_ref.at[:, pl.ds(length - EDGE, EDGE)], before, y_send.at[1], y_recv.at[1], device(net, wide, up))
     to_down.start()
     to_up.start()
-    mains = []
-    for dn, dw in offsets:
+    def hand_on(src, ref, dn, dw, send, recv):
+        slot = dn * wides + lax.rem(dw + wides - 1 + 2 * core, wides)
+        return remote(src, ref.at[slot], send.at[slot], recv.at[slot], partner)
+
+    mains, sent = [], []
+    for dn, dw in direct:
         slot = dn * wides + dw
         mains.append(remote(own_ref, main_ref.at[slot], main_send.at[slot], main_recv.at[slot], target(dn, dw)))
         mains[-1].start()
+    sent.append(hand_on(own_ref, main_ref, 0, 0, main_send, main_recv))
+    sent[-1].start()
     own_main = pltpu.make_async_copy(own_ref, main_ref.at[0], local_sem.at[0])
     own_main.start()
     to_down.wait()
@@ -101,19 +120,32 @@
         lane < EDGE // 2, after[...].astype(jnp.float32), before[...].astype(jnp.float32)
     ).astype(packed.dtype)
     edges = []
-    for dn, dw in offsets:
+    for dn, dw in direct:
         slot = dn * wides + dw
         edges.append(remote(packed, edge_ref.at[slot], edge_send.at[slot], edge_recv.at[slot], target(dn, dw)))
         edges[-1].start()
+    sent.append(hand_on(packed, edge_ref, 0, 0, edge_send, edge_recv))
+    sent[-1].start()
     own_edge = pltpu.make_async_copy(packed, edge_ref.at[0], local_sem.at[1])
     own_edge.start()
     joined_weights(conv1_ref, conv2_ref, pick1_ref, pick2_ref, tile_ref, w1_ref, w2_ref, big_z)
-    for copy in mains + edges + [own_main, own_edge]:
-        copy.wait()
+    for copies, ref, send, recv in ((mains, main_ref, main_send, main_recv), (edges, edge_ref, edge_send, edge_recv)):
+        for copy, (dn, dw) in zip(copies, direct):
+            copy.wait_recv()
+            sent.append(hand_on(ref.at[dn * wides + dw], ref, dn, dw, send, recv))
+            sent[-1].start()
+    for copy in mains + edges + sent:
+        copy.wait_send()
+    for slot in handed:
+        remote(main_ref.at[slot], main_ref.at[slot], main_send.at[slot], main_recv.at[slot], partner).wait_recv()
+        remote(edge_ref.at[slot], edge_ref.at[slot], edge_send.at[slot], edge_recv.at[slot], partner).wait_recv()
+    own_main.wait()
+    own_edge.wait()
 
 
 def gather(own, conv1, conv2, picks, width, big_z, nets, wides, narrows):
-    rows, length = own.shape
+    count, depth, xs, length = own.shape
+    rows = count * depth * xs
     travel = jnp.bfloat16
     columns = picks[2].shape[1]
     slots = nets * wides
@@ -124,9 +156,10 @@
             jax.ShapeDtypeStruct((slots, rows, EDGE), travel),
             jax.ShapeDtypeStruct((picks[0].shape[0], 3, picks[0].shape[1], columns), jnp.bfloat16),
             jax.ShapeDtypeStruct((3, columns, 3 * width), jnp.bfloat16),
+            jax.ShapeDtypeStruct((count, xs, depth, length), jnp.float32),
         ],
         in_specs=[pl.BlockSpec(memory_space=pltpu.VMEM)] * 6,
-        out_specs=[pl.BlockSpec(memory_space=pl.ANY)] * 2 + [pl.BlockSpec(memory_space=pltpu.VMEM)] * 2,
+        out_specs=[pl.BlockSpec(memory_space=pl.ANY)] * 2 + [pl.BlockSpec(memory_space=pltpu.VMEM)] * 3,
         scratch_shapes=[
             pltpu.VMEM((rows, length), travel),
             pltpu.VMEM((rows, EDGE), travel),
@@ -348,7 +381,7 @@
     for x in range(xs):
         def give(c, q, rate):
             moved = (q + TIME_STEP * rate)[:depth, :lanes]
-            out_ref[c, x] = own_ref[c, x] * (1.0 / 3.0) + (2.0 / 3.0) * moved
+            out_ref[c, :, x, :] = own_ref[c, x] * (1.0 / 3.0) + (2.0 / 3.0) * moved
 
         rates(base, x, give)
 
@@ -364,7 +397,7 @@
     channels, width = w2.shape[1], w2.shape[2] // 3
     return pl.pallas_call(
         functools.partial(step_kernel, nets, wides),
-        out_shape=jax.ShapeDtypeStruct(own.shape, jnp.float32),
+        out_shape=jax.ShapeDtypeStruct((fields, depth, xs, lanes), jnp.float32),
         in_specs=[pl.BlockSpec(memory_space=pl.ANY)] * 2 + [pl.BlockSpec(memory_space=pltpu.VMEM)] * 6,
         out_specs=pl.BlockSpec(memory_space=pltpu.VMEM),
         scratch_shapes=[
@@ -423,14 +456,12 @@
     big_z = depth * nets
     hidden, parts = conv1_weight.shape[1], conv2_weight.shape[1]
     pool, spread, *picks = constants(lanes, big_z, count, hidden, parts)
-    own = fields.transpose(0, 2, 1, 3)
-    main, edge, w1, w2 = gather(
-        own.reshape(-1, lanes), conv1_weight.transpose(0, 2, 1), conv2_weight, picks,
+    main, edge, w1, w2, own = gather(
+        fields, conv1_weight.transpose(0, 2, 1), conv2_weight.transpose(1, 0, 2), picks,
         picks[1].shape[0] // 3, big_z, nets, wides, narrows,
     )
     bias = conv1_bias[None]
-    moved = step(main, edge, own, w1, bias, w2, pool, spread, nets, wides)
-    return moved.transpose(0, 2, 1, 3)
+    return step(main, edge, own, w1, bias, w2, pool, spread, nets, wides)
 
 
 def solution(mesh):

time: 42.3 us -> 35.8 us (0.85)
  local copies, waits for them, and re-layouts: 4.63 us -> 0 us
  Pallas kernels: 37.4 us -> 35.6 us
    unnamed x2 -> x0, local copies, waits for them, and re-layouts: 3.02 us -> none
    pallas_call x1, Pallas kernels: 18.5 us -> 16.6 us  [gather(): pl.pallas_call(functools.partial(gather_kernel, nets, wides, narrows, big...]
    transpose x1 -> x0, local copies, waits for them, and re-layouts: 1.61 us -> none  [per_device(): return moved.transpose(0, 2, 1, 3)]
where the time goes in v2:
time: 35.8 us; the launch traced here: 35.6 us
  Pallas kernels  35.6 us (99%)
    pallas_call x1, Pallas kernels, step(): pl.pallas_call(functools.partial(step_kernel, nets, wides), out_shape=jax...  18.9 us
    pallas_call x1, Pallas kernels, gather(): pl.pallas_call(functools.partial(gather_kernel, nets, wides, narrows, big...  16.6 us

profile of v2, /device:TPU:0, one launch (start us, length us, event | category | flops | bytes accessed | tf_op | source)
XLA Modules:
  0.0 35.6 jit_solution(3251312466262047870)
XLA Ops:
  0.0 16.6 %shard_map.91 = (bf16[8,128,256]{2,1,0:T(8,128)(2,1)}, bf16[8,128,128]{2,1,0:T(8,128)(2,1)}, bf16[2,3,256,256]{3,2,1,0:T(8,128)(2,1)}, bf16[3,256,192]{2,1,0:T(8,128)(2,1)}, f32[4,4,8,256]{3,2,1,0:T(8,128)}) custom-call(f32[4,8,4,256]{3,2,1,0:T(4,128)} %state_ref.1, bf16[27,4,32]{2,1,0:T(4,128)(2,1)} %bitcast.4, bf16[6,27,32]{2,1,0:T(8,128)(2,1)} %bitcast.3, ...), custom_call_target="tpu_custom_call" | custom-call | tf_op jit(solution)/shard_map/pallas_call | solution.py:152
  16.6 18.9 %shard_map.92 = f32[4,8,4,256]{3,2,1,0:T(4,128)} custom-call(bf16[8,128,256]{2,1,0:T(8,128)(2,1)} %get-tuple-element.10.main_ref, bf16[8,128,128]{2,1,0:T(8,128)(2,1)} %get-tuple-element.11.edge_ref, f32[4,4,8,256]{3,2,1,0:T(8,128)} %get-tuple-element.12.own_ref, bf16[2,3,256,256]{3,2,1,0:T(8,128)(2,1)} %get-tuple-element.13.w1_ref, f32[1,32]{1,0:T(1,128)} %bitcast.5, ...), custom_call_target="tpu_custom_call" | custom-call | tf_op jit(solution)/shard_map/pallas_call | solution.py:398

commit v3 on v2

--- a/solution.py
+++ b/solution.py
@@ -42,7 +42,7 @@
     def second_tap(t):
         return jnp.concatenate([second[i, t : t + 1] for i in range(second.shape[0])], axis=0)
 
-    for dy in range(3):
+    def build(dy):
         total = [None] * w1_ref.shape[0]
         for dz in range(3):
             spread = jnp.dot(stacked(lambda t: conv1_ref[t].astype(f32), dz, dy), tile, preferred_element_type=f32).astype(bf16)
@@ -60,6 +60,8 @@
             value = term if dz == 0 else value + term
         w2_ref[dy] = value.astype(bf16)
 
+    return build
+
 
 def gather_kernel(nets, wides, narrows, big_z, state_ref, conv1_ref, conv2_ref, pick1_ref, pick2_ref, tile_ref,
                   main_ref, edge_ref, w1_ref, w2_ref, turned_ref, own_ref, after, before, packed,
@@ -113,6 +115,8 @@
     sent[-1].start()
     own_main = pltpu.make_async_copy(own_ref, main_ref.at[0], local_sem.at[0])
     own_main.start()
+    build = joined_weights(conv1_ref, conv2_ref, pick1_ref, pick2_ref, tile_ref, w1_ref, w2_ref, big_z)
+    build(0)
     to_down.wait()
     to_up.wait()
     lane = lax.broadcasted_iota(jnp.int32, after.shape, 1)
@@ -128,12 +132,14 @@
     sent[-1].start()
     own_edge = pltpu.make_async_copy(packed, edge_ref.at[0], local_sem.at[1])
     own_edge.start()
-    joined_weights(conv1_ref, conv2_ref, pick1_ref, pick2_ref, tile_ref, w1_ref, w2_ref, big_z)
+    build(1)
     for copies, ref, send, recv in ((mains, main_ref, main_send, main_recv), (edges, edge_ref, edge_send, edge_recv)):
         for copy, (dn, dw) in zip(copies, direct):
             copy.wait_recv()
             sent.append(hand_on(ref.at[dn * wides + dw], ref, dn, dw, send, recv))
             sent[-1].start()
+        if ref is main_ref:
+            build(2)
     for copy in mains + edges + sent:
         copy.wait_send()
     for slot in handed:
@@ -244,7 +250,12 @@
     def wrapped(i, size):
         return (i + size) % size if isinstance(i, int) else lax.rem(i + size, size)
 
-    def forces(src):
+    def forces(src, last=False):
+        own_x = xs // 2
+        whole = batch < coarse_x or not last
+        inner = [x for x in range(coarse_x) if whole or (x + 2) % coarse_x < own_x + 4]
+        outer = [x for x in range(coarse_x) if whole or (x + 1) % coarse_x < own_x + 2]
+
         @functools.partial(each, coarse_x // part_x)
         def _(turn):
             chunk = turn * part_x
@@ -279,7 +290,7 @@
         def _(turn):
             begin = turn * batch
             for variant in range(variants):
-                mine = list(range(variant, batch, variants))
+                mine = [x for x in range(variant, batch, variants) if batch < coarse_x or x in inner]
                 rows = []
                 for x in mine:
                     at = pl.multiple_of(begin * block + (pad + (x - 1) * block) // 128 * 128, 128)
@@ -293,16 +304,19 @@
                     for dy in range(3):
                         moved = (here if dy == 1 else shifted(here, dy - 1, 0)).astype(jnp.bfloat16)
                         wide_hidden[x, :, pl.ds(dy * channels, channels)] = moved
+            used = range(batch) if batch < coarse_x else inner
             found = jnp.dot(
-                wide_hidden[...].reshape(batch * coarse_ring, 3 * channels),
+                jnp.concatenate([wide_hidden[x] for x in used], axis=0),
                 w2_ref[...].reshape(3 * channels, 3 * width),
                 preferred_element_type=jnp.float32,
             )
-            found = found.reshape(batch, coarse_ring, 3 * width)
+            found = found.reshape(len(used), coarse_ring, 3 * width)
             for i in range(batch):
                 if batch == coarse_x:
-                    total = found[(i - 1) % coarse_x, :, :width] + found[i, :, width : 2 * width]
-                    partial[i] = total + found[(i + 1) % coarse_x, :, 2 * width :]
+                    if i in outer:
+                        left, here, right = [inner.index((i + d) % coarse_x) for d in (-1, 0, 1)]
+                        total = found[left, :, :width] + found[here, :, width : 2 * width]
+                        partial[i] = total + found[right, :, 2 * width :]
                 else:
                     for dx in range(3):
                         partial[wrapped(begin + i + 1 - dx, coarse_x)] += found[i, :, dx * width : (dx + 1) * width]
@@ -315,7 +329,8 @@
 
         if batch == coarse_x:
             for x in range(0, coarse_x, together):
-                turn_over(x)
+                if any(x + i in outer for i in range(together)):
+                    turn_over(x)
         else:
             pl.loop(0, coarse_x // together)(lambda i: turn_over(i * together))
 
@@ -328,7 +343,7 @@
             )
             upper[pl.ds(begin, batch)] = fine.reshape(batch, width, ring)
 
-        @pl.loop(0, coarse_x, unroll=unroll)
+        @pl.loop(0, own_x if last else coarse_x, unroll=unroll)
         def _(x):
             ahead, behind = wrapped(x + 1, coarse_x), wrapped(x - 1, coarse_x)
 
@@ -376,7 +391,7 @@
 
         rates(state, x, give)
 
-    forces(base)
+    forces(base, last=True)
 
     for x in range(xs):
         def give(c, q, rate):

time: 35.8 us -> 34.4 us (0.961)
  Pallas kernels: 35.6 us -> 34.2 us
    pallas_call x1, Pallas kernels: 18.9 us -> 18 us  [step(): pl.pallas_call(functools.partial(step_kernel, nets, wides), out_shape=jax...]
    pallas_call x1, Pallas kernels: 16.6 us -> 16.3 us  [gather(): pl.pallas_call(functools.partial(gather_kernel, nets, wides, narrows, big...]
where the time goes in v3:
time: 34.4 us; the launch traced here: 34.2 us
  Pallas kernels  34.2 us (99%)
    pallas_call x1, Pallas kernels, step(): pl.pallas_call(functools.partial(step_kernel, nets, wides), out_shape=jax...  18 us
    pallas_call x1, Pallas kernels, gather(): pl.pallas_call(functools.partial(gather_kernel, nets, wides, narrows, big...  16.3 us

profile of v3, /device:TPU:0, one launch (start us, length us, event | category | flops | bytes accessed | tf_op | source)
XLA Modules:
  0.0 34.2 jit_solution(15674961282161592737)
XLA Ops:
  0.0 16.3 %shard_map.91 = (bf16[8,128,256]{2,1,0:T(8,128)(2,1)}, bf16[8,128,128]{2,1,0:T(8,128)(2,1)}, bf16[2,3,256,256]{3,2,1,0:T(8,128)(2,1)}, bf16[3,256,192]{2,1,0:T(8,128)(2,1)}, f32[4,4,8,256]{3,2,1,0:T(8,128)}) custom-call(f32[4,8,4,256]{3,2,1,0:T(4,128)} %state_ref.1, bf16[27,4,32]{2,1,0:T(4,128)(2,1)} %bitcast.4, bf16[6,27,32]{2,1,0:T(8,128)(2,1)} %bitcast.3, ...), custom_call_target="tpu_custom_call" | custom-call | tf_op jit(solution)/shard_map/pallas_call | solution.py:158
  16.3 18.0 %shard_map.92 = f32[4,8,4,256]{3,2,1,0:T(4,128)} custom-call(bf16[8,128,256]{2,1,0:T(8,128)(2,1)} %get-tuple-element.10.main_ref, bf16[8,128,128]{2,1,0:T(8,128)(2,1)} %get-tuple-element.11.edge_ref, f32[4,4,8,256]{3,2,1,0:T(8,128)} %get-tuple-element.12.own_ref, bf16[2,3,256,256]{3,2,1,0:T(8,128)(2,1)} %get-tuple-element.13.w1_ref, f32[1,32]{1,0:T(1,128)} %bitcast.5, ...), custom_call_target="tpu_custom_call" | custom-call | tf_op jit(solution)/shard_map/pallas_call | solution.py:413

commit v4 on v3

--- a/solution.py
+++ b/solution.py
@@ -375,7 +375,7 @@
 
     forces(base)
 
-    @pl.loop(0, big_x, unroll=unroll)
+    @pl.loop(0, big_x, unroll=2 * unroll if unroll > 1 else 1)
     def _(x):
         def give(c, q, rate):
             state[c, x] = q + TIME_STEP * rate
@@ -384,7 +384,7 @@
 
     forces(state)
 
-    @pl.loop(0, big_x, unroll=unroll)
+    @pl.loop(0, big_x, unroll=2 * unroll if unroll > 1 else 1)
     def _(x):
         def give(c, q, rate):
             base[c, x] = 0.75 * base[c, x] + 0.25 * (q + TIME_STEP * rate)

time: 34.4 us -> 34.2 us (level)
  no operation moved by 1% of the time
where the time goes in v4:
time: 34.2 us; the launch traced here: 34 us
  Pallas kernels  34 us (99%)
    pallas_call x1, Pallas kernels, step(): pl.pallas_call(functools.partial(step_kernel, nets, wides), out_shape=jax...  17.7 us
    pallas_call x1, Pallas kernels, gather(): pl.pallas_call(functools.partial(gather_kernel, nets, wides, narrows, big...  16.3 us

profile of v4, /device:TPU:0, one launch (start us, length us, event | category | flops | bytes accessed | tf_op | source)
XLA Modules:
  0.0 34.0 jit_solution(10702653659359486120)
XLA Ops:
  0.0 16.3 %shard_map.91 = (bf16[8,128,256]{2,1,0:T(8,128)(2,1)}, bf16[8,128,128]{2,1,0:T(8,128)(2,1)}, bf16[2,3,256,256]{3,2,1,0:T(8,128)(2,1)}, bf16[3,256,192]{2,1,0:T(8,128)(2,1)}, f32[4,4,8,256]{3,2,1,0:T(8,128)}) custom-call(f32[4,8,4,256]{3,2,1,0:T(4,128)} %state_ref.1, bf16[27,4,32]{2,1,0:T(4,128)(2,1)} %bitcast.4, bf16[6,27,32]{2,1,0:T(8,128)(2,1)} %bitcast.3, ...), custom_call_target="tpu_custom_call" | custom-call | tf_op jit(solution)/shard_map/pallas_call | solution.py:158
  16.3 17.7 %shard_map.92 = f32[4,8,4,256]{3,2,1,0:T(4,128)} custom-call(bf16[8,128,256]{2,1,0:T(8,128)(2,1)} %get-tuple-element.10.main_ref, bf16[8,128,128]{2,1,0:T(8,128)(2,1)} %get-tuple-element.11.edge_ref, f32[4,4,8,256]{3,2,1,0:T(8,128)} %get-tuple-element.12.own_ref, bf16[2,3,256,256]{3,2,1,0:T(8,128)(2,1)} %get-tuple-element.13.w1_ref, f32[1,32]{1,0:T(1,128)} %bitcast.5, ...), custom_call_target="tpu_custom_call" | custom-call | tf_op jit(solution)/shard_map/pallas_call | solution.py:413
